TPU v7x, 32 devices: a whole 2x2x4 slice. The times are simulated.
32 devices in a mesh: groups: 2 (over x), dp: 2 (over core), tensor: 8 (over z, y).
Axes of the slice: x: 2, y: 2, z: 4, core: 2. Of those that a mesh axis runs over, the one named last changes fastest.
Arguments:
- incoming_patches: bfloat16 [4, 128, 1280], P(('groups', 'dp'), 'tensor'), parts along dimension 0, may hold values from -6 to 6
- patch_ranking: int32 [4, 128], P(('groups', 'dp')), parts along dimension 0, may hold values from 0 to 127, each once within a row
- tier_quotas: int32 [4, 4], P(('groups', 'dp')), parts along dimension 0, may hold values from 1 to 64, 128 in all within a row
- standardize_scaling: float32 [1280], replicated, may hold values from 0.1 to 1.9
- expand_matrix: bfloat16 [1280, 5120], P(None, 'tensor'), may hold values from -0.15625 to 0.15625
- contract_matrix: bfloat16 [5120, 1280], P('tensor'), may hold values from -0.078125 to 0.078125
- upstream_adjoint: bfloat16 [4, 128, 1280], P(('groups', 'dp'), 'tensor'), parts along dimension 0, may hold values from -6 to 6
Outputs:
- block_out: bfloat16 [4, 128, 1280], P(('groups', 'dp'), 'tensor'), parts along dimension 0
- grad_input: bfloat16 [4, 128, 1280], P(('groups', 'dp'), 'tensor'), parts along dimension 0
- grad_weight_in: float32 [2560, 5120], P('groups', 'tensor'), parts along dimension 0
- grad_weight_out: float32 [10240, 1280], P(('groups', 'tensor')), parts along dimension 0
- grad_gain: float32 [2560], P('groups'), parts along dimension 0
There are 2 independent parts, one for each index of `groups`. A program takes and returns all parts, laid end to end along the dimension named above; an argument that names none is the same for every part. Nothing has to cross between parts.
Inputs may be any that keep to these rules, and one draw needn't show every extreme that they name: `patch_ranking`: each clip's ranks are a permutation of 0 to 127. `tier_quotas`: each clip's four capacities sum to 128.
All inputs are finite; a program needn't handle non-finite values.
Results may differ from a plain program's by a relative error of at most 0.0057.
Values may be sent and summed in bfloat16 or wider, within the bound.
A program may use at most 64 MiB of HBM per device.

v0:
```python
from functools import partial

import jax
import jax.numpy as jnp
from jax import lax
from jax.sharding import PartitionSpec as P

D = 1280
FF = 5120


def patch_tiers(patch_ranking, tier_quotas):
    hindmost_tier = tier_quotas[:, 3]
    central_tier = hindmost_tier + tier_quotas[:, 2]
    foremost_tier = central_tier + tier_quotas[:, 1]
    matryoshka_tier = (patch_ranking < hindmost_tier[:, None]).astype(jnp.int32)
    matryoshka_tier = matryoshka_tier + (patch_ranking < central_tier[:, None]).astype(jnp.int32)
    matryoshka_tier = matryoshka_tier + (patch_ranking < foremost_tier[:, None]).astype(jnp.int32)
    return matryoshka_tier


def norm_rows(rows_float, width_limit, standardize_scaling):
    column = lax.broadcasted_iota(jnp.int32, rows_float.shape, 1)
    inside = column < width_limit[:, None]
    entries = width_limit.astype(jnp.float32)[:, None]
    average = jnp.sum(jnp.where(inside, rows_float, 0.0), axis=1, keepdims=True) / entries
    centred = jnp.where(inside, rows_float - average, 0.0)
    variance = jnp.sum(centred * centred, axis=1, keepdims=True) / entries
    return centred * lax.rsqrt(variance + 1e-06) * standardize_scaling[None, :]


def shards(
    incoming_patches,
    patch_ranking,
    tier_quotas,
    standardize_scaling,
    expand_matrix,
    contract_matrix,
    upstream_adjoint,
):
    own_rows = incoming_patches.shape[1]
    model_width = incoming_patches.shape[2]
    hid_shard = expand_matrix.shape[1]
    position = lax.axis_index("tensor")
    shot_tier_breadth = patch_tiers(patch_ranking, tier_quotas).reshape(-1)
    level_own = lax.dynamic_slice_in_dim(shot_tier_breadth, position * own_rows, own_rows)
    hid_clip = FF // 8 * jnp.left_shift(jnp.ones_like(shot_tier_breadth), shot_tier_breadth)
    dim_own = D // 8 * jnp.left_shift(jnp.ones_like(level_own), level_own)
    token_rows = incoming_patches.reshape(own_rows, model_width)
    grad_rows = upstream_adjoint.reshape(own_rows, model_width)
    col_own = lax.broadcasted_iota(jnp.int32, (1, model_width), 1) < dim_own[:, None]
    out_grad_own = jnp.where(col_own, grad_rows, jnp.zeros_like(grad_rows))
    normed_float, norm_back = jax.vjp(
        lambda rows_float, gain_vec: norm_rows(rows_float, dim_own, gain_vec),
        token_rows.astype(jnp.float32),
        standardize_scaling,
    )
    hid_column = position * hid_shard + lax.broadcasted_iota(jnp.int32, (1, hid_shard), 1)
    hid_mask = hid_column < hid_clip[:, None]
    normed_own = normed_float.astype(jnp.bfloat16)
    normed, out_grad = (
        lax.all_gather(normed_own, "tensor", axis=0, tiled=True),
        lax.all_gather(out_grad_own, "tensor", axis=0, tiled=True),
    )
    preact = jnp.dot(normed, expand_matrix, preferred_element_type=jnp.float32)
    gelu_value, gelu_back = jax.vjp(partial(jax.nn.gelu, approximate=False), preact)
    hidden = jnp.where(hid_mask, gelu_value, 0.0).astype(jnp.bfloat16)
    picked = lax.slice_in_dim(hidden, 0, own_rows * lax.axis_size("tensor"), axis=0)
    projected = lax.psum_scatter(
        jnp.dot(picked, contract_matrix, preferred_element_type=jnp.float32),
        "tensor",
        scatter_dimension=0,
        tiled=True,
    )
    block_out = (token_rows.astype(jnp.float32) + jnp.where(col_own, projected, 0.0)).astype(
        jnp.bfloat16
    )
    hidden_grad = jnp.dot(out_grad, contract_matrix.T, preferred_element_type=jnp.float32)
    preact_grad = jnp.where(hid_mask, gelu_back(hidden_grad)[0], 0.0).astype(jnp.bfloat16)
    local_out_grad = jnp.dot(hidden.T, out_grad, preferred_element_type=jnp.float32)
    local_in_grad = jnp.dot(normed.T, preact_grad, preferred_element_type=jnp.float32)
    picked = preact_grad
    normed_grad = lax.psum_scatter(
        jnp.dot(picked, expand_matrix.T, preferred_element_type=jnp.float32),
        "tensor",
        scatter_dimension=0,
        tiled=True,
    )
    grad_weight_in, grad_weight_out = lax.psum((local_in_grad, local_out_grad), "dp")
    input_part, local_gain = norm_back(normed_grad)
    grad_gain = lax.psum(local_gain, ("dp", "tensor"))
    grad_input = (grad_rows.astype(jnp.float32) + input_part).astype(jnp.bfloat16)
    return (
        block_out.reshape(incoming_patches.shape),
        grad_input.reshape(incoming_patches.shape),
        grad_weight_in,
        grad_weight_out,
        grad_gain,
    )


def solution(mesh):
    return jax.shard_map(
        shards,
        mesh=mesh,
        in_specs=(
            P(("groups", "dp"), "tensor", None),
            P(("groups", "dp"), None),
            P(("groups", "dp"), None),
            P(),
            P(None, "tensor"),
            P("tensor", None),
            P(("groups", "dp"), "tensor", None),
        ),
        out_specs=(
            P(("groups", "dp"), "tensor", None),
            P(("groups", "dp"), "tensor", None),
            P("groups", "tensor"),
            P(("groups", "tensor"), None),
            P("groups"),
        ),
        check_vma=False,
    )
```

profile of v0, /device:TPU:0, one launch (start us, length us, event | category | flops | bytes accessed | tf_op | source)
XLA Modules:
  0.0 228.7 jit_solution(9195746593662781520)
XLA Ops:
  8.1 1.4 fusion.30
  11.4 1.3 multiply_bitcast_fusion
  12.8 1.0 fusion.9
  13.8 1.0 fusion.15
  14.9 0.9 fusion.18
  15.8 32.6 %all_gather.7 = bf16[128,1280]{1,0:T(8,128)(2,1)S(1)} all-gather(bf16[16,1280]{1,0:T(8,128)(2,1)S(1)} %fusion.18), channel_id=1, replica_groups=mesh['groups'=2,'dp'=2,'tensor'=8] {'tensor'}, dimensions={0}, use_global_device_ids=true | all-gather | bytes 368640 | tf_op jit(solution)/shard_map/all_gather | solution.py:63
  48.4 0.9 multiply_convert_fusion
  49.3 30.9 %all_gather.6 = bf16[128,1280]{1,0:T(8,128)(2,1)S(1)} all-gather(bf16[16,1280]{1,0:T(8,128)(2,1)S(1)} %multiply_convert_fusion), channel_id=1, replica_groups=mesh['groups'=2,'dp'=2,'tensor'=8] {'tensor'}, dimensions={0}, use_global_device_ids=true | all-gather | bytes 368640 | tf_op jit(solution)/shard_map/all_gather | solution.py:62
  80.1 1.9 fusion.31
  82.0 1.2 fusion.1
  83.2 0.2 copy-done.1
  83.4 1.4 fusion.33
  84.9 0.1 fusion
  85.0 1.3 fusion.32
  86.4 2.3 %fusion.34 = f32[1280,640]{1,0:T(8,128)} fusion(bf16[128,1280]{1,0:T(8,128)(2,1)S(1)} %all_gather.6, bf16[128,640]{1,0:T(8,128)(2,1)S(1)} %get-tuple-element.11), kind=kOutput, calls=%fused_computation.59 | convolution fusion | flops 209715200 | bytes 3768320 | tf_op jit(solution)/shard_map/dot_general | solution.py:81
  88.7 2.3 %fusion.35 = f32[640,1280]{1,0:T(8,128)} fusion(bf16[128,640]{1,0:T(8,128)(2,1)S(1)} %fusion, bf16[128,1280]{1,0:T(8,128)(2,1)S(1)} %all_gather.7), kind=kOutput, calls=%fused_computation.60 | convolution fusion | flops 209715200 | bytes 3768320 | tf_op jit(solution)/shard_map/dot_general | solution.py:80
  91.1 57.0 %reduce-scatter.5.cloned.1.call-done = f32[16,1280]{1,0:T(8,128)} async-done(((f32[128,1280]{1,0:T(8,128)}), f32[16,1280]{1,0:T(8,128)}) %reduce-scatter.5.cloned.1.call-update) | async-done | bytes 81936 | tf_op jit(solution)/shard_map/reduce_scatter | solution.py:83
  148.1 1.1 multiply_reduce_fusion
  149.2 32.2 %psum.23 = f32[1280]{0:T(1024)} all-reduce(f32[1280]{0:T(1024)S(1)} %get-tuple-element.5), channel_id=1, replica_groups=mesh['groups'=2,'dp'=2,'tensor'=8] {'dp','tensor'}, use_global_device_ids=true, to_apply=%region_9.10 | all-reduce | flops 1280 | bytes 10240 | tf_op jit(solution)/shard_map/psum | solution.py:91
  181.5 31.5 %reduce-scatter.3.cloned.1.call-done = f32[16,1280]{1,0:T(8,128)} async-done(((f32[128,1280]{1,0:T(8,128)}), f32[16,1280]{1,0:T(8,128)}) %reduce-scatter.3.cloned.1.call-update) | async-done | bytes 81936 | tf_op jit(solution)/shard_map/reduce_scatter | solution.py:69
  213.0 1.8 fusion.24
  214.8 0.7 fusion.19
  215.6 4.0 %copy.14 = f32[1280,640]{1,0:T(8,128)} copy(f32[1280,640]{1,0:T(8,128)} %get-tuple-element.23) | data formatting | bytes 6553600
  219.5 1.7 copy.15
  (24 shorter events, 0.6 us)
Async XLA Ops:
  8.0 74.0 %copy-start = (bf16[640,1280]{1,0:T(8,128)(2,1)S(1)}, bf16[640,1280]{1,0:T(8,128)(2,1)}, u32[]{:S(2)}) copy-start(bf16[640,1280]{1,0:T(8,128)(2,1)} %param.12) | copy-start | bytes 4915204
  8.0 140.1 %reduce-scatter.5.cloned.1.call-start = ((), (), s32[]{:S(2)}) async-start(), calls=%async_computation.3 | async-start | bytes 737280 | tf_op jit(solution)/shard_map/reduce_scatter | solution.py:83
  82.0 1.4 copy-start.1
  84.9 128.1 %reduce-scatter.3.cloned.1.call-start = ((), (), s32[]{:S(2)}) async-start(), calls=%async_computation.2 | async-start | bytes 737280 | tf_op jit(solution)/shard_map/reduce_scatter | solution.py:69
  86.3 129.2 %all-reduce.3.cloned.1.call-start = ((), (), s32[]{:S(2)}) async-start(), calls=%async_computation.4 | async-start | bytes 13107200 | tf_op jit(solution)/shard_map/psum | solution.py:89
  91.0 57.1 %copy-start.3 = (bf16[1,16,1280]{2,1,0:T(8,128)(2,1)S(1)}, bf16[1,16,1280]{2,1,0:T(8,128)(2,1)}, u32[]{:S(2)}) copy-start(bf16[1,16,1280]{2,1,0:T(8,128)(2,1)} %param.7) | copy-start | bytes 122884
  91.1 57.1 %copy-start.5 = (f32[1280]{0:T(1024)S(1)}, f32[1280]{0:T(1024)}, u32[]{:S(2)}) copy-start(f32[1280]{0:T(1024)} %param.10) | copy-start | bytes 15364
  91.1 123.8 %copy-start.4 = (bf16[1,16,1280]{2,1,0:T(8,128)(2,1)S(1)}, bf16[1,16,1280]{2,1,0:T(8,128)(2,1)}, u32[]{:S(2)}) copy-start(bf16[1,16,1280]{2,1,0:T(8,128)(2,1)} %param.13) | copy-start | bytes 122884
  215.5 4.0 %copy-start.2 = (f32[640,1280]{1,0:T(8,128)S(1)}, f32[640,1280]{1,0:T(8,128)}, u32[]{:S(2)}) copy-start(f32[640,1280]{1,0:T(8,128)} %get-tuple-element.24) | copy-start | bytes 9830404
Sparse Core Ops, SparseCore 0:
  85.0 63.0 reduce-scatter.4
  151.8 61.2 reduce-scatter.2
Sparse Core Ops, SparseCore 1:
  91.2 33.1 all-reduce.2
where the time goes:
time: 229 us
  blocking collectives  95.7 us (42%)
  waiting for transfers between devices  88.6 us (39%)
  between operations  17.5 us (8%)
  matrix products  10.4 us (5%)
  other arithmetic  9.04 us (4%)
  local copies, waits for them, and re-layouts  7.33 us (3%)
    reduce_scatter x1, waiting for transfers between devices, shards(): lax.psum_scatter(jnp.dot(picked, expand_matrix.T, preferred_element_type=...  57 us
    all_gather x1, blocking collectives, shards(): lax.all_gather(out_grad_own, 'tensor', axis=0, tiled=True)  32.6 us
    psum x1, blocking collectives, shards(): grad_gain = lax.psum(local_gain, ('dp', 'tensor'))  32.2 us
    reduce_scatter x1, waiting for transfers between devices, shards(): lax.psum_scatter(jnp.dot(picked, contract_matrix, preferred_element_type=...  31.5 us
    all_gather x1, blocking collectives, shards(): lax.all_gather(normed_own, 'tensor', axis=0, tiled=True)  30.9 us
    unnamed x14, local copies, waits for them, and re-layouts  5.94 us
  transfers between devices with their start and end apart: 3, of which 2 were waited for; matrix products, arithmetic and copies ran while one was open for 4% of the time, Pallas kernels for 0%

commit v1 on v0

v1 whole, which is shorter than its diff:
```python
from functools import partial

import jax
import jax.numpy as jnp
from jax import lax
from jax.experimental import pallas as pl
from jax.experimental.pallas import tpu as pltpu
from jax.sharding import PartitionSpec as P

D = 1280
FF = 5120
MESH = pl.DeviceIdType.MESH


def each(count, body, start=0):
    if count - start <= 16:
        for i in range(start, count):
            body(i)
    else:
        lax.fori_loop(start, count, lambda i, c: (body(i), c)[1], 0)


def block_kernel(
    n,
    inner,
    x_ref,
    up_ref,
    rank_ref,
    quota_ref,
    gain_ref,
    w1_hbm,
    w2_hbm,
    out_ref,
    gin_ref,
    ggain_ref,
    normed_ref,
    ograd_ref,
    hid_ref,
    pgrad_ref,
    w1_ref,
    w2_ref,
    pre_ref,
    part_ref,
    ybuf_ref,
    sum_ref,
    zbuf_ref,
    own_ref,
    gparts_ref,
    w_sem,
    gz_send,
    gy_send,
    g_recv,
    ry_send,
    ry_recv,
    rz_send,
    rz_recv,
    gg_send,
    gg_recv,
    dp_send,
    dp_recv,
):
    outer = n // inner
    rows_own = x_ref.shape[1]
    tokens = n * rows_own
    width = x_ref.shape[2]
    hid = w1_ref.shape[1]
    me = lax.axis_index("tensor")
    dp = lax.axis_index("dp")
    z = me // inner
    y = me % inner
    turn = 1 - 2 * (z // max(outer // 2, 1))
    slot = dp * n + me

    def z_at(k):
        return (z + turn * k + outer) % outer

    def y_at(j):
        return (y + j) % inner

    def rows(t):
        return pl.ds(pl.multiple_of(t * rows_own, rows_own), rows_own)

    load_w1 = pltpu.make_async_copy(w1_hbm, w1_ref, w_sem.at[0])
    load_w2 = pltpu.make_async_copy(w2_hbm, w2_ref, w_sem.at[1])
    load_w1.start()
    load_w2.start()

    barrier = pltpu.get_barrier_semaphore()

    def greet(q):
        t = (slot + q) % (2 * n)
        pl.semaphore_signal(
            barrier, inc=1, device_id={"tensor": t % n, "dp": t // n}, device_id_type=MESH
        )

    each(2 * n, greet, 1)

    narrow3 = quota_ref[0, 3]
    narrow2 = narrow3 + quota_ref[0, 2]
    narrow1 = narrow2 + quota_ref[0, 1]
    rank = rank_ref[...]
    factor_row = (
        1.0
        + jnp.where(rank < narrow1, 1.0, 0.0)
        + jnp.where(rank < narrow2, 2.0, 0.0)
        + jnp.where(rank < narrow3, 4.0, 0.0)
    )

    def factor_of(first, count):
        token = first + lax.broadcasted_iota(jnp.int32, (count, tokens), 0)
        lane = lax.broadcasted_iota(jnp.int32, (count, tokens), 1)
        return jnp.sum(jnp.where(token == lane, factor_row, 0.0), axis=1, keepdims=True)

    entries = (D // 8) * factor_of(me * rows_own, rows_own)
    column = lax.broadcasted_iota(jnp.int32, (rows_own, width), 1).astype(jnp.float32)
    inside = column < entries
    gain = gain_ref[...]
    x = x_ref[0].astype(jnp.float32)
    up = up_ref[0].astype(jnp.float32)
    average = jnp.sum(jnp.where(inside, x, 0.0), axis=1, keepdims=True) / entries
    centred = jnp.where(inside, x - average, 0.0)
    variance = jnp.sum(centred * centred, axis=1, keepdims=True) / entries
    scale = lax.rsqrt(variance + 1e-06)
    xhat = centred * scale
    gathered = (normed_ref, ograd_ref)
    normed_ref[dp, rows(me), :] = (xhat * gain).astype(jnp.bfloat16)
    ograd_ref[dp, rows(me), :] = jnp.where(inside, up, 0.0).astype(jnp.bfloat16)

    pl.semaphore_wait(barrier, 2 * n - 1)

    def move(c, t, target, send):
        block = gathered[c].at[dp, rows(t), :]
        return pltpu.make_async_remote_copy(
            src_ref=block,
            dst_ref=block,
            send_sem=send,
            recv_sem=g_recv.at[c, t],
            device_id={"tensor": target},
            device_id_type=MESH,
        )

    def z_move(c, k):
        return move(c, me, z_at(k) * inner + y, gz_send.at[c, k])

    def y_move(c, k, j):
        return move(c, z_at(k) * inner + y, z * inner + y_at(j), gy_send.at[c, k, j])

    def landed(c, t):
        move(c, t, me, gz_send.at[c, 0]).wait_recv()

    for c in range(2):
        each(outer, lambda k: z_move(c, k).start(), 1)
        each(inner, lambda j: y_move(c, 0, j).start(), 1)

    def relay(c, k):
        landed(c, z_at(k) * inner + y)
        each(inner, lambda j: y_move(c, k, j).start(), 1)

    for c in range(2):
        each(outer, lambda k: relay(c, k), 1)

    def arrive(c):
        each(
            outer,
            lambda k: each(inner, lambda j: landed(c, z_at(k) * inner + y_at(j)), 1),
        )

    def across(index, ref):
        return pltpu.make_async_remote_copy(
            src_ref=ref.at[dp],
            dst_ref=ref.at[dp],
            send_sem=dp_send.at[index],
            recv_sem=dp_recv.at[index],
            device_id={"dp": 1 - dp},
            device_id_type=MESH,
        )

    chunk = min(tokens, 128)
    hid_column = (me * hid + lax.broadcasted_iota(jnp.int32, (chunk, hid), 1)).astype(jnp.float32)

    def hid_inside(r):
        return hid_column < (FF // 8) * factor_of(r * chunk, chunk)

    def at(r):
        return pl.ds(pl.multiple_of(r * chunk, chunk), chunk)

    def dot(a, b, contract_b):
        return lax.dot_general(
            a, b, (((1,), (contract_b,)), ((), ())), preferred_element_type=jnp.float32
        )

    def forward(r):
        preact = dot(normed_ref[dp, at(r), :], w1_ref[...], 0)
        cdf = 0.5 * (1.0 + lax.erf(preact * 0.7071067811865476))
        density = jnp.exp(-0.5 * preact * preact) * 0.3989422804014327
        ok = hid_inside(r)
        hidden = jnp.where(ok, preact * cdf, 0.0).astype(jnp.bfloat16)
        pre_ref[at(r), :] = jnp.where(ok, cdf + preact * density, 0.0)
        hid_ref[dp, at(r), :] = hidden
        part_ref[0, at(r), :] = dot(hidden, w2_ref[...], 0).astype(jnp.bfloat16)

    def backward(r, total):
        hidden_grad = dot(ograd_ref[dp, at(r), :], w2_ref[...], 1)
        preact_grad = (pre_ref[at(r), :] * hidden_grad).astype(jnp.bfloat16)
        pgrad_ref[dp, at(r), :] = preact_grad
        normed_grad = dot(preact_grad, w1_ref[...], 1)
        part_ref[1, at(r), :] = normed_grad.astype(jnp.bfloat16)
        weighted = normed_grad * normed_ref[dp, at(r), :].astype(jnp.float32)
        return total + jnp.sum(weighted, axis=0, keepdims=True)

    def y_sum(c, k, j):
        return pltpu.make_async_remote_copy(
            src_ref=part_ref.at[c, rows(z_at(k) * inner + y_at(j)), :],
            dst_ref=ybuf_ref.at[c, k, j],
            send_sem=ry_send.at[c, k, j],
            recv_sem=ry_recv.at[c, k, j],
            device_id={"tensor": z * inner + y_at(j)},
            device_id_type=MESH,
        )

    def z_sum(c, k):
        return pltpu.make_async_remote_copy(
            src_ref=sum_ref.at[c, k],
            dst_ref=zbuf_ref.at[c, z],
            send_sem=rz_send.at[c, k],
            recv_sem=rz_recv.at[c, z],
            device_id={"tensor": z_at(k) * inner + y},
            device_id_type=MESH,
        )

    def z_landed(c, k):
        return pltpu.make_async_remote_copy(
            src_ref=sum_ref.at[c, k],
            dst_ref=zbuf_ref.at[c, z_at(k)],
            send_sem=rz_send.at[c, k],
            recv_sem=rz_recv.at[c, z_at(k)],
            device_id={"tensor": z_at(k) * inner + y},
            device_id_type=MESH,
        )

    def spread(c):
        each(outer, lambda k: each(inner, lambda j: y_sum(c, k, j).start(), 1), 1)
        each(inner, lambda j: y_sum(c, 0, j).start(), 1)

    def inner_total(c, k):
        total = part_ref[c, rows(z_at(k) * inner + y), :].astype(jnp.float32)
        for j in range(1, inner):
            y_sum(c, k, j).wait_recv()
            total = total + ybuf_ref[c, k, j].astype(jnp.float32)
        return total

    def pass_on(c, k):
        sum_ref[c, k] = inner_total(c, k).astype(jnp.bfloat16)
        z_sum(c, k).start()

    def outer_total(c):
        own_ref[...] = inner_total(c, 0)

        def add(k):
            z_landed(c, k).wait_recv()
            own_ref[...] += zbuf_ref[c, z_at(k)].astype(jnp.float32)

        each(outer, add, 1)
        return own_ref[...]

    def gain_move(q):
        t = (slot + q) % (2 * n)
        return pltpu.make_async_remote_copy(
            src_ref=gparts_ref.at[slot],
            dst_ref=gparts_ref.at[slot],
            send_sem=gg_send.at[q],
            recv_sem=gg_recv.at[slot],
            device_id={"tensor": t % n, "dp": t // n},
            device_id_type=MESH,
        )

    def gain_landed(q):
        t = (slot + q) % (2 * n)
        pltpu.make_async_remote_copy(
            src_ref=gparts_ref.at[t],
            dst_ref=gparts_ref.at[t],
            send_sem=gg_send.at[q],
            recv_sem=gg_recv.at[t],
            device_id={"tensor": t % n, "dp": t // n},
            device_id_type=MESH,
        ).wait_recv()

    load_w1.wait()
    load_w2.wait()
    arrive(0)
    each(tokens // chunk, forward)
    spread(0)
    arrive(1)
    zero = jnp.zeros((1, width), jnp.float32)
    if tokens == chunk:
        gain_part = backward(0, zero)
    else:
        gain_part = lax.fori_loop(0, tokens // chunk, backward, zero)
    spread(1)
    gparts_ref[slot] = gain_part / gain
    each(outer, lambda k: pass_on(0, k), 1)
    each(2 * n, lambda q: gain_move(q).start(), 1)
    everything = (normed_ref, ograd_ref, hid_ref, pgrad_ref)
    for index, ref in enumerate(everything):
        across(index, ref).start()
    each(outer, lambda k: pass_on(1, k), 1)

    projected = outer_total(0)
    out_ref[0] = (x + jnp.where(inside, projected, 0.0)).astype(jnp.bfloat16)

    each(2 * n, gain_landed, 1)
    own_ref[0:1, :] = gparts_ref[0]

    def add_gain(t):
        own_ref[0:1, :] += gparts_ref[t]

    each(2 * n, add_gain, 1)
    ggain_ref[...] = own_ref[0:1, :]

    lifted = jnp.where(inside, outer_total(1) * gain, 0.0)
    mean_lifted = jnp.sum(lifted, axis=1, keepdims=True) / entries
    mean_along = jnp.sum(lifted * xhat, axis=1, keepdims=True) / entries
    input_part = scale * (lifted - mean_lifted - xhat * mean_along)
    gin_ref[0] = (up + jnp.where(inside, input_part, 0.0)).astype(jnp.bfloat16)

    for index, ref in enumerate(everything):
        across(index, ref).wait()
    for c in range(2):
        each(outer, lambda k: z_move(c, k).wait_send(), 1)
        each(outer, lambda k: each(inner, lambda j: y_move(c, k, j).wait_send(), 1))
        each(outer, lambda k: each(inner, lambda j: y_sum(c, k, j).wait_send(), 1))
        each(outer, lambda k: z_sum(c, k).wait_send(), 1)
    each(2 * n, lambda q: gain_move(q).wait_send(), 1)


def shards(
    n,
    incoming_patches,
    patch_ranking,
    tier_quotas,
    standardize_scaling,
    expand_matrix,
    contract_matrix,
    upstream_adjoint,
):
    rows_own, width = incoming_patches.shape[1:]
    tokens = n * rows_own
    hid = expand_matrix.shape[1]
    inner = 2 ** ((n.bit_length() - 1) // 2)
    outer = n // inner
    bf16, f32 = jnp.bfloat16, jnp.float32
    vmem = pl.BlockSpec(memory_space=pltpu.VMEM)
    dma = pltpu.SemaphoreType.DMA
    block_out, grad_input, grad_gain, normed, out_grad, hidden, preact_grad = pl.pallas_call(
        partial(block_kernel, n, inner),
        out_shape=(
            jax.ShapeDtypeStruct(incoming_patches.shape, bf16),
            jax.ShapeDtypeStruct(incoming_patches.shape, bf16),
            jax.ShapeDtypeStruct((1, width), f32),
            jax.ShapeDtypeStruct((2, tokens, width), bf16),
            jax.ShapeDtypeStruct((2, tokens, width), bf16),
            jax.ShapeDtypeStruct((2, tokens, hid), bf16),
            jax.ShapeDtypeStruct((2, tokens, hid), bf16),
        ),
        in_specs=[
            vmem,
            vmem,
            vmem,
            pl.BlockSpec(memory_space=pltpu.SMEM),
            vmem,
            pl.BlockSpec(memory_space=pl.ANY),
            pl.BlockSpec(memory_space=pl.ANY),
        ],
        out_specs=(vmem,) * 7,
        scratch_shapes=[
            pltpu.VMEM((width, hid), bf16),
            pltpu.VMEM((hid, width), bf16),
            pltpu.VMEM((tokens, hid), f32),
            pltpu.VMEM((2, tokens, width), bf16),
            pltpu.VMEM((2, outer, inner, rows_own, width), bf16),
            pltpu.VMEM((2, outer, rows_own, width), bf16),
            pltpu.VMEM((2, outer, rows_own, width), bf16),
            pltpu.VMEM((rows_own, width), f32),
            pltpu.VMEM((2 * n, 1, width), f32),
            dma((2,)),
            dma((2, outer)),
            dma((2, outer, inner)),
            dma((2, n)),
            dma((2, outer, inner)),
            dma((2, outer, inner)),
            dma((2, outer)),
            dma((2, outer)),
            dma((2 * n,)),
            dma((2 * n,)),
            dma((4,)),
            dma((4,)),
        ],
        compiler_params=pltpu.CompilerParams(
            collective_id=0, has_side_effects=True, vmem_limit_bytes=56 * 1024 * 1024
        ),
    )(
        incoming_patches,
        upstream_adjoint,
        patch_ranking,
        tier_quotas,
        standardize_scaling.reshape(1, width),
        expand_matrix,
        contract_matrix,
    )
    both = lambda a: a.reshape(2 * tokens, a.shape[2])
    grad_weight_in = jnp.dot(both(normed).T, both(preact_grad), preferred_element_type=f32)
    grad_weight_out = jnp.dot(both(hidden).T, both(out_grad), preferred_element_type=f32)
    return block_out, grad_input, grad_weight_in, grad_weight_out, grad_gain.reshape(width)


def solution(mesh):
    return jax.shard_map(
        partial(shards, mesh.shape["tensor"]),
        mesh=mesh,
        in_specs=(
            P(("groups", "dp"), "tensor", None),
            P(("groups", "dp"), None),
            P(("groups", "dp"), None),
            P(),
            P(None, "tensor"),
            P("tensor", None),
            P(("groups", "dp"), "tensor", None),
        ),
        out_specs=(
            P(("groups", "dp"), "tensor", None),
            P(("groups", "dp"), "tensor", None),
            P("groups", "tensor"),
            P(("groups", "tensor"), None),
            P("groups"),
        ),
        check_vma=False,
    )
```

time: 229 us -> 42.5 us (0.19)
  blocking collectives: 95.7 us -> 0 us
  waiting for transfers between devices: 88.6 us -> 0 us
  Pallas kernels: 0 us -> 32.4 us
  between operations: 17.5 us -> 0.68 us
  other arithmetic: 9.04 us -> 0.62 us
  local copies, waits for them, and re-layouts: 7.33 us -> 2.55 us
  matrix products: 10.4 us -> 6.03 us
    reduce_scatter x2 -> x0, waiting for transfers between devices: 88.5 us -> none  [the longest x1 57 us: shards(): lax.psum_scatter(jnp.dot(picked, expand_matrix.T, preferred_element_type=...]
    all_gather x2 -> x0, blocking collectives: 63.5 us -> none  [the longest x1 32.6 us: shards(): lax.all_gather(out_grad_own, 'tensor', axis=0, tiled=True)]
    pallas_call x0 -> x1, Pallas kernels: none -> 32.4 us  [shards(): pl.pallas_call(partial(block_kernel, n, inner), out_shape=(jax.ShapeDtype...]
    psum x1 -> x0, blocking collectives: 32.2 us -> none  [shards(): grad_gain = lax.psum(local_gain, ('dp', 'tensor'))]
    reduce_sum x4 -> x0, other arithmetic: 4.8 us -> none  [the longest x1 1.75 us: norm_rows(): centred = jnp.where(inside, rows_float - average, 0.0)]
    unnamed x14 -> x12, local copies, waits for them, and re-layouts: 5.94 us -> 1.26 us
    dot_general x6 -> x2, matrix products: 10.4 us -> 6.03 us  [the longest x1 3.61 us: shards(): jnp.dot(both(hidden).T, both(out_grad), preferred_element_type=f32)]
  transfers between devices with their start and end apart: 3 -> 0, of which waited for: 2 -> 0; matrix products, arithmetic and copies ran while one was open for 4% -> 0% of each run, Pallas kernels for 0% -> 0%
where the time goes in v1:
time: 42.5 us; the launch traced here: 42.3 us
  Pallas kernels  32.4 us (76%)
  matrix products  6.03 us (14%)
  local copies, waits for them, and re-layouts  2.55 us (6%)
  between operations  0.68 us (2%)
  other arithmetic  0.62 us (1%)
    pallas_call x1, Pallas kernels, shards(): pl.pallas_call(partial(block_kernel, n, inner), out_shape=(jax.ShapeDtype...  32.4 us
    dot_general x1, matrix products, shards(): jnp.dot(both(hidden).T, both(out_grad), preferred_element_type=f32)  3.61 us
    dot_general x1, matrix products, shards(): jnp.dot(both(normed).T, both(preact_grad), preferred_element_type=f32)  2.42 us
    reshape x1, local copies, waits for them, and re-layouts, shards(): standardize_scaling.reshape(1, width)  1.29 us
    unnamed x12, local copies, waits for them, and re-layouts  1.26 us

profile of v1, /device:TPU:0, one launch (start us, length us, event | category | flops | bytes accessed | tf_op | source)
XLA Modules:
  0.0 42.3 jit_solution(12296949636508203921)
XLA Ops:
  0.6 1.3 %reshape.15.gain_ref = f32[1,1280]{1,0:T(1,128)} reshape(f32[1280]{0:T(1024)} %param.10) | data formatting | bytes 10240 | tf_op jit(solution)/shard_map/reshape | solution.py:406
  1.9 32.4 %shard_map.110 = (bf16[1,16,1280]{2,1,0:T(8,128)(2,1)}, bf16[1,16,1280]{2,1,0:T(8,128)(2,1)}, f32[1,1280]{1,0:T(1,128)}, bf16[2,128,1280]{2,1,0:T(8,128)(2,1)}, ...) custom-call(bf16[1,16,1280]{2,1,0:T(8,128)(2,1)} %x_ref.1, ...), custom_call_target="tpu_custom_call" | custom-call | tf_op jit(solution)/shard_map/pallas_call | solution.py:354
  34.3 0.0 copy-start
  34.3 0.0 copy-start.1
  34.3 0.0 copy-start.4
  34.3 0.0 copy-start.3
  34.3 0.0 copy-start.2
  34.4 3.6 %convolution_bitcast_fusion = f32[640,1280]{1,0:T(8,128)} fusion(bf16[2,128,640]{2,1,0:T(8,128)(2,1)} %get-tuple-element.16, bf16[2,128,1280]{2,1,0:T(8,128)(2,1)} %get-tuple-element.17), kind=kOutput, calls=%fused_computation | convolution fusion | flops 419430400 | bytes 4259840 | tf_op jit(solution)/shard_map/dot_general | solution.py:412
  38.0 0.0 copy-done
  38.0 0.0 copy-done.1
  38.0 2.4 %convolution_bitcast_fusion.1 = f32[1280,640]{1,0:T(8,128)} fusion(bf16[2,128,1280]{2,1,0:T(8,128)(2,1)S(1)} %copy-done, bf16[2,128,640]{2,1,0:T(8,128)(2,1)S(1)} %copy-done.1), kind=kOutput, calls=%fused_computation.1 | convolution fusion | flops 419430400 | bytes 4259840 | tf_op jit(solution)/shard_map/dot_general | solution.py:411
  40.4 0.0 copy-done.4
  40.4 0.6 %reduce = f32[1280]{0:T(1024)} reduce(f32[1,1280]{1,0:T(1,128)S(1)} %copy-done.4, f32[]{:T(128)} %constant.4), dimensions={0}, to_apply=%get-tuple-element.18.reduce_sub_computation | reduce | bytes 10244 | tf_op jit(solution)/shard_map/pallas_call | solution.py:354
  41.0 0.0 copy-done.3
  41.0 0.6 %copy.18 = bf16[1,16,1280]{2,1,0:T(8,128)(2,1)} copy(bf16[1,16,1280]{2,1,0:T(8,128)(2,1)S(1)} %copy-done.3) | data formatting | bytes 81920
  41.6 0.0 copy-done.2
  41.6 0.6 %copy.19 = bf16[1,16,1280]{2,1,0:T(8,128)(2,1)} copy(bf16[1,16,1280]{2,1,0:T(8,128)(2,1)S(1)} %copy-done.2) | data formatting | bytes 81920
Async XLA Ops:
  34.3 3.7 %copy-start = (bf16[2,128,1280]{2,1,0:T(8,128)(2,1)S(1)}, bf16[2,128,1280]{2,1,0:T(8,128)(2,1)}, u32[]{:S(2)}) copy-start(bf16[2,128,1280]{2,1,0:T(8,128)(2,1)} %get-tuple-element.14) | copy-start | bytes 1966084
  34.3 3.7 %copy-start.1 = (bf16[2,128,640]{2,1,0:T(8,128)(2,1)S(1)}, bf16[2,128,640]{2,1,0:T(8,128)(2,1)}, u32[]{:S(2)}) copy-start(bf16[2,128,640]{2,1,0:T(8,128)(2,1)} %get-tuple-element.15) | copy-start | bytes 983044
  34.3 6.1 %copy-start.4 = (f32[1,1280]{1,0:T(1,128)S(1)}, f32[1,1280]{1,0:T(1,128)}, u32[]{:S(2)}) copy-start(f32[1,1280]{1,0:T(1,128)} %get-tuple-element.18) | copy-start | bytes 15364
  34.3 6.7 %copy-start.3 = (bf16[1,16,1280]{2,1,0:T(8,128)(2,1)S(1)}, bf16[1,16,1280]{2,1,0:T(8,128)(2,1)}, u32[]{:S(2)}) copy-start(bf16[1,16,1280]{2,1,0:T(8,128)(2,1)} %get-tuple-element.24) | copy-start | bytes 122884
  34.3 7.3 %copy-start.2 = (bf16[1,16,1280]{2,1,0:T(8,128)(2,1)S(1)}, bf16[1,16,1280]{2,1,0:T(8,128)(2,1)}, u32[]{:S(2)}) copy-start(bf16[1,16,1280]{2,1,0:T(8,128)(2,1)} %get-tuple-element.25) | copy-start | bytes 122884

commit v2 on v1

--- a/solution.py
+++ b/solution.py
@@ -33,6 +33,8 @@
     out_ref,
     gin_ref,
     ggain_ref,
+    gw1_ref,
+    gw2_ref,
     normed_ref,
     ograd_ref,
     hid_ref,
@@ -114,7 +116,7 @@
     entries = (D // 8) * factor_of(me * rows_own, rows_own)
     column = lax.broadcasted_iota(jnp.int32, (rows_own, width), 1).astype(jnp.float32)
     inside = column < entries
-    gain = gain_ref[...]
+    gain = gain_ref[...].reshape(1, width)
     x = x_ref[0].astype(jnp.float32)
     up = up_ref[0].astype(jnp.float32)
     average = jnp.sum(jnp.where(inside, x, 0.0), axis=1, keepdims=True) / entries
@@ -285,25 +287,51 @@
             device_id_type=MESH,
         ).wait_recv()
 
+    everything = (normed_ref, ograd_ref, hid_ref, pgrad_ref)
+
+    def share(index):
+        across(index, everything[index]).start()
+
+    def clips(index, columns):
+        a = everything[index][:, :, columns]
+        return a.reshape(2 * tokens, a.shape[2])
+
+    def weight_grad(target, left, right):
+        across(left, everything[left]).wait_recv()
+        across(right, everything[right]).wait_recv()
+        height = target.shape[0]
+        step = 128 if height % 128 == 0 else height
+        b = clips(right, slice(None))
+        for first in range(0, height, step):
+            target[first : first + step, :] = lax.dot_general(
+                clips(left, slice(first, first + step)),
+                b,
+                (((0,), (0,)), ((), ())),
+                preferred_element_type=jnp.float32,
+            )
+
     load_w1.wait()
     load_w2.wait()
     arrive(0)
+    share(0)
     each(tokens // chunk, forward)
     spread(0)
+    share(2)
     arrive(1)
+    share(1)
     zero = jnp.zeros((1, width), jnp.float32)
     if tokens == chunk:
         gain_part = backward(0, zero)
     else:
         gain_part = lax.fori_loop(0, tokens // chunk, backward, zero)
     spread(1)
+    share(3)
+    each(outer, lambda k: pass_on(0, k), 1)
     gparts_ref[slot] = gain_part / gain
-    each(outer, lambda k: pass_on(0, k), 1)
     each(2 * n, lambda q: gain_move(q).start(), 1)
-    everything = (normed_ref, ograd_ref, hid_ref, pgrad_ref)
-    for index, ref in enumerate(everything):
-        across(index, ref).start()
+    weight_grad(gw2_ref, 2, 1)
     each(outer, lambda k: pass_on(1, k), 1)
+    weight_grad(gw1_ref, 0, 3)
 
     projected = outer_total(0)
     out_ref[0] = (x + jnp.where(inside, projected, 0.0)).astype(jnp.bfloat16)
@@ -315,7 +343,7 @@
         own_ref[0:1, :] += gparts_ref[t]
 
     each(2 * n, add_gain, 1)
-    ggain_ref[...] = own_ref[0:1, :]
+    ggain_ref[...] = own_ref[0:1, :].reshape(width)
 
     lifted = jnp.where(inside, outer_total(1) * gain, 0.0)
     mean_lifted = jnp.sum(lifted, axis=1, keepdims=True) / entries
@@ -324,13 +352,25 @@
     gin_ref[0] = (up + jnp.where(inside, input_part, 0.0)).astype(jnp.bfloat16)
 
     for index, ref in enumerate(everything):
-        across(index, ref).wait()
+        across(index, ref).wait_send()
     for c in range(2):
         each(outer, lambda k: z_move(c, k).wait_send(), 1)
         each(outer, lambda k: each(inner, lambda j: y_move(c, k, j).wait_send(), 1))
         each(outer, lambda k: each(inner, lambda j: y_sum(c, k, j).wait_send(), 1))
         each(outer, lambda k: z_sum(c, k).wait_send(), 1)
     each(2 * n, lambda q: gain_move(q).wait_send(), 1)
+
+
+def store_kernel(*refs):
+    sem = refs[-1]
+    half = (len(refs) - 1) // 2
+    copies = [
+        pltpu.make_async_copy(refs[i], refs[half + i], sem.at[i]) for i in range(half)
+    ]
+    for copy in copies:
+        copy.start()
+    for copy in copies:
+        copy.wait()
 
 
 def shards(
@@ -351,17 +391,16 @@
     bf16, f32 = jnp.bfloat16, jnp.float32
     vmem = pl.BlockSpec(memory_space=pltpu.VMEM)
     dma = pltpu.SemaphoreType.DMA
-    block_out, grad_input, grad_gain, normed, out_grad, hidden, preact_grad = pl.pallas_call(
+    out_types = (
+        (incoming_patches.shape, bf16),
+        (incoming_patches.shape, bf16),
+        ((width,), f32),
+        ((width, hid), f32),
+        ((hid, width), f32),
+    )
+    results = pl.pallas_call(
         partial(block_kernel, n, inner),
-        out_shape=(
-            jax.ShapeDtypeStruct(incoming_patches.shape, bf16),
-            jax.ShapeDtypeStruct(incoming_patches.shape, bf16),
-            jax.ShapeDtypeStruct((1, width), f32),
-            jax.ShapeDtypeStruct((2, tokens, width), bf16),
-            jax.ShapeDtypeStruct((2, tokens, width), bf16),
-            jax.ShapeDtypeStruct((2, tokens, hid), bf16),
-            jax.ShapeDtypeStruct((2, tokens, hid), bf16),
-        ),
+        out_shape=tuple(pltpu.VMEM(*t) for t in out_types),
         in_specs=[
             vmem,
             vmem,
@@ -371,8 +410,12 @@
             pl.BlockSpec(memory_space=pl.ANY),
             pl.BlockSpec(memory_space=pl.ANY),
         ],
-        out_specs=(vmem,) * 7,
+        out_specs=(vmem,) * 5,
         scratch_shapes=[
+            pltpu.VMEM((2, tokens, width), bf16),
+            pltpu.VMEM((2, tokens, width), bf16),
+            pltpu.VMEM((2, tokens, hid), bf16),
+            pltpu.VMEM((2, tokens, hid), bf16),
             pltpu.VMEM((width, hid), bf16),
             pltpu.VMEM((hid, width), bf16),
             pltpu.VMEM((tokens, hid), f32),
@@ -403,14 +446,19 @@
         upstream_adjoint,
         patch_ranking,
         tier_quotas,
-        standardize_scaling.reshape(1, width),
+        standardize_scaling,
         expand_matrix,
         contract_matrix,
     )
-    both = lambda a: a.reshape(2 * tokens, a.shape[2])
-    grad_weight_in = jnp.dot(both(normed).T, both(preact_grad), preferred_element_type=f32)
-    grad_weight_out = jnp.dot(both(hidden).T, both(out_grad), preferred_element_type=f32)
-    return block_out, grad_input, grad_weight_in, grad_weight_out, grad_gain.reshape(width)
+    block_out, grad_input, grad_gain, grad_weight_in, grad_weight_out = pl.pallas_call(
+        store_kernel,
+        out_shape=tuple(jax.ShapeDtypeStruct(*t) for t in out_types),
+        in_specs=[vmem] * 5,
+        out_specs=(pl.BlockSpec(memory_space=pl.ANY),) * 5,
+        scratch_shapes=[dma((5,))],
+        compiler_params=pltpu.CompilerParams(vmem_limit_bytes=56 * 1024 * 1024),
+    )(*(pltpu.with_memory_space_constraint(r, pltpu.VMEM) for r in results))
+    return block_out, grad_input, grad_weight_in, grad_weight_out, grad_gain
 
 
 def solution(mesh):

time: 42.5 us -> 35.1 us (0.83)
  matrix products: 6.03 us -> 0 us
  local copies, waits for them, and re-layouts: 2.55 us -> 0 us
  Pallas kernels: 32.4 us -> 34.3 us
  other arithmetic: 0.62 us -> 0 us
    dot_general x2 -> x0, matrix products: 6.03 us -> none  [the longest x1 3.61 us: shards(): jnp.dot(both(hidden).T, both(out_grad), preferred_element_type=f32)]
    pallas_call x1 -> x2, Pallas kernels: 32.4 us -> 34.3 us  [the longest x1 31.4 us: shards(): pl.pallas_call(partial(block_kernel, n, inner), out_shape=tuple((pltpu.VM...]
    reshape x1 -> x0, local copies, waits for them, and re-layouts: 1.29 us -> none  [shards(): standardize_scaling.reshape(1, width)]
    unnamed x12 -> x0, local copies, waits for them, and re-layouts: 1.26 us -> none
    pallas_call x1 -> x0, other arithmetic: 0.62 us -> none  [shards(): pl.pallas_call(partial(block_kernel, n, inner), out_shape=(jax.ShapeDtype...]
where the time goes in v2:
time: 35.1 us; the launch traced here: 34.9 us
  Pallas kernels  34.3 us (98%)
  between operations  0.64 us (2%)
    pallas_call x1, Pallas kernels, shards(): pl.pallas_call(partial(block_kernel, n, inner), out_shape=tuple((pltpu.VM...  31.4 us
    pallas_call x1, Pallas kernels, shards(): pl.pallas_call(store_kernel, out_shape=tuple((jax.ShapeDtypeStruct(*t) fo...  2.86 us

profile of v2, /device:TPU:0, one launch (start us, length us, event | category | flops | bytes accessed | tf_op | source)
XLA Modules:
  0.0 34.9 jit_solution(3921678913150720734)
XLA Ops:
  0.6 31.4 %shard_map.110 = (bf16[1,16,1280]{2,1,0:T(8,128)(2,1)S(1)}, bf16[1,16,1280]{2,1,0:T(8,128)(2,1)S(1)}, f32[1280]{0:T(1024)S(1)}, f32[1280,640]{1,0:T(8,128)S(1)}, f32[640,1280]{1,0:T(8,128)S(1)}) custom-call(bf16[1,16,1280]{2,1,0:T(8,128)(2,1)} %x_ref.1, bf16[1,16,1280]{2,1,0:T(8,128)(2,1)} %up_ref.1, s32[1,128]{1,0:T(1,128)} %rank_ref.1, s32[1,4]{1,0:T(1,128)} %quota_ref.1, ...), custom_call_target="tpu_custom_call" | custom-call | tf_op jit(solution)/shard_map/pallas_call | solution.py:401
  32.0 2.9 %shard_map.111 = (bf16[1,16,1280]{2,1,0:T(8,128)(2,1)}, bf16[1,16,1280]{2,1,0:T(8,128)(2,1)}, f32[1280]{0:T(1024)}, f32[1280,640]{1,0:T(8,128)}, f32[640,1280]{1,0:T(8,128)}) custom-call(bf16[1,16,1280]{2,1,0:T(8,128)(2,1)S(1)} %get-tuple-element.15.refs_0_, bf16[1,16,1280]{2,1,0:T(8,128)(2,1)S(1)} %get-tuple-element.16.refs_1_, ...), custom_call_target="tpu_custom_call" | custom-call | tf_op jit(solution)/shard_map/pallas_call | solution.py:453
